TPU v7x, 256 devices: a whole 4x4x8 slice. The times are simulated.
256 devices in a mesh: row: 64 (over y, x_hi, z), ch: 4 (over x_lo, core).
Axes of the slice: x: 4 (x_hi: 2, x_lo: 2; x = x_hi * 2 + x_lo), y: 4, z: 8, core: 2. Of those that a mesh axis runs over, the one named last changes fastest.
Arguments:
- pair_field: bfloat16 [128, 512, 512], P('ch', 'row'), may hold values from -25 to 25
- input_gain: float32 [128], replicated, may hold values from 0.5 to 1.5
- input_bias: float32 [128], replicated, may hold values from -1.2 to 1.2
- left_weight: bfloat16 [128, 128], P(None, 'ch'), may hold values from -0.5 to 0.5
- left_gate: bfloat16 [128, 128], P(None, 'ch'), may hold values from -0.5 to 0.5
- right_weight: bfloat16 [128, 128], P(None, 'ch'), may hold values from -0.5 to 0.5
- right_gate: bfloat16 [128, 128], P(None, 'ch'), may hold values from -0.5 to 0.5
- gate_weight: bfloat16 [128, 128], P(None, 'ch'), may hold values from -0.5 to 0.5
- output_gain: float32 [128], replicated, may hold values from 0.5 to 1.5
- output_bias: float32 [128], replicated, may hold values from -1.2 to 1.2
- final_weight: bfloat16 [128, 128], P(None, 'ch'), may hold values from -0.5 to 0.5
Outputs:
- transposed: bfloat16 [128, 512, 512], P('ch', 'row')
All inputs are finite; a program needn't handle non-finite values.
Results may differ from a plain program's by a relative error of at most 0.012.
Values may be sent and summed in bfloat16 or wider, within the bound.
No kernel may reach another device: no remote copies, remote signals or barrier semaphores. Data moves between devices by JAX's collectives and lax.ppermute only.
A program may use at most 64 MiB of HBM per device.

v0:
```python
import jax
import jax.numpy as jnp
from jax import lax
from jax.sharding import PartitionSpec as P

epsilon = 1e-05


def layer_norm(values, gain, bias):
    average = jnp.mean(values, axis=-2, keepdims=True)
    centred = values - average
    variance = jnp.mean(centred * centred, axis=-2, keepdims=True)
    return centred * lax.rsqrt(variance + epsilon) * gain[:, None] + bias[:, None]


def swap(array, step):
    return lax.ppermute(array, "ch", [(s, s ^ step) for s in range(4)])


def place(blocks, mine):
    stacked = jnp.stack(blocks)
    return jnp.stack([lax.dynamic_index_in_dim(stacked, mine ^ t, 0, False) for t in range(4)])


def body(
    pair_field,
    input_gain,
    input_bias,
    left_weight,
    left_gate,
    right_weight,
    right_gate,
    gate_weight,
    output_gain,
    output_bias,
    final_weight,
):
    mine = lax.axis_index("ch")
    core = mine % 2
    everyone = ("row", "ch")
    weights = jnp.concatenate(
        [w.T for w in (left_weight, left_gate, right_weight, right_gate)], axis=1
    )
    late = lax.all_gather(
        jnp.concatenate([gate_weight.T, final_weight.T], axis=1), "ch", axis=0, tiled=True
    )
    field = jnp.swapaxes(pair_field, 0, 1)

    def message(step):
        part = lax.dynamic_slice(field, (2 * (mine ^ step), 0, 0), (2, 32, 512))
        return jnp.concatenate([part.reshape(64, 512), weights], axis=0)

    got = place([message(0)] + [swap(message(t), t) for t in (1, 2, 3)], mine)
    whole = jnp.swapaxes(got[:, :64].reshape(4, 2, 32, 512), 0, 1).reshape(2, 128, 512)
    wide = got[:, 64:].reshape(128, 4, 128)
    normed = layer_norm(whole.astype(jnp.float32), input_gain, input_bias).astype(jnp.bfloat16)

    def project(weight):
        return jnp.einsum("dc,ack->dak", weight, normed, preferred_element_type=jnp.float32)

    left = jax.nn.sigmoid(project(wide[:, 1])) * project(wide[:, 0])
    right = jax.nn.sigmoid(project(wide[:, 3])) * project(wide[:, 2])
    sent = jnp.concatenate([left.reshape(256, 4, 128), right.reshape(256, 4, 128)], axis=1).astype(
        jnp.bfloat16
    )
    factors = lax.all_to_all(sent, everyone, 0, 0, tiled=True)
    other = swap(factors[:, :4], 1)
    own = factors[:, :4].reshape(256, 512)
    other = other.reshape(256, 512)
    rows = jnp.stack([jnp.where(core == 0, own, other), jnp.where(core == 0, other, own)], axis=1)
    product = jnp.einsum(
        "jk,ik->ji",
        factors[:, 4:].reshape(256, 512),
        rows.reshape(512, 512),
        preferred_element_type=jnp.float32,
    ).astype(jnp.bfloat16)
    gating = jax.nn.sigmoid(
        jnp.einsum("ec,acj->jae", late[:, :128], normed, preferred_element_type=jnp.float32)
    ).astype(jnp.bfloat16)
    sent = jnp.concatenate([product.reshape(256, 4, 128), gating.reshape(256, 4, 128)], axis=1)
    got = lax.all_to_all(sent, everyone, 0, 0, tiled=True)
    hidden = jnp.swapaxes(got[:, :4].reshape(128, 2, 512), 0, 1)
    normed = layer_norm(hidden.astype(jnp.float32), output_gain, output_bias).astype(jnp.bfloat16)
    update = jnp.einsum("ed,jdi->jei", late[:, 128:], normed, preferred_element_type=jnp.float32)
    gating = got[:, 4:].reshape(256, 2, 2, 128).transpose(1, 3, 0, 2).reshape(2, 128, 512)
    update = (update * gating.astype(jnp.float32)).astype(jnp.bfloat16)

    def part(step):
        return lax.dynamic_slice(update, (0, 32 * (mine ^ step), 0), (2, 32, 512))

    got = place([part(0)] + [swap(part(t), t) for t in (1, 2, 3)], mine)
    return jnp.swapaxes(got.reshape(8, 32, 512), 0, 1)


def solution(mesh):
    placed = (
        P("ch", "row", None),
        P(),
        P(),
        P(None, "ch"),
        P(None, "ch"),
        P(None, "ch"),
        P(None, "ch"),
        P(None, "ch"),
        P(),
        P(),
        P(None, "ch"),
    )
    return jax.shard_map(
        body, mesh=mesh, in_specs=placed, out_specs=P("ch", "row", None), check_vma=False
    )
```

profile of v0, /device:TPU:1, one launch (start us, length us, event | category | flops | bytes accessed | tf_op | source)
XLA Modules:
  0.0 90.2 jit_solution(11001124090783543311)
XLA Ops:
  0.0 1.7 %constant_dynamic-slice_fusion.14 = (bf16[32,2,512]{2,1,0:T(2,128)(2,1)S(1)}, bf16[32,2,512]{2,1,0:T(2,128)(2,1)S(1)}, bf16[32,2,512]{2,1,0:T(2,128)(2,1)S(1)}, bf16[32,2,512]{2,1,0:T(2,128)(2,1)S(1)}) fusion(bf16[32,8,512]{2,1,0:T(8,128)(2,1)} %param.11, s32[]{:T(128)S(6)} %select_n.81, s32[]{:T(128)S(6)} %select_n.83, s32[]{:T(128)S(6)} %select_n.82, ...), kind=kLoop, calls=%fused_computation.85 | loop fusion | bytes 524304 | tf_op jit(solution)/shard_map/dynamic-slice
  1.8 0.6 copy-done.1
  2.5 3.3 %collective-permute-start = (bf16[96,512]{1,0:T(8,128)(2,1)S(1)}, bf16[96,512]{1,0:T(8,128)(2,1)S(1)}, u32[]{:S(2)}, u32[]{:S(2)}) collective-permute-start(bf16[96,512]{1,0:T(8,128)(2,1)S(1)} %get-tuple-element.33), channel_id=1, source_target_pairs={{0,1},{1,0},{2,3},{3,2},{4,5},{5,4},{6,7},{7,6},{8,9},{9,8},{10,11... | collective-permute-start | bytes 294920 | tf_op jit(solution)/shard_map/ppermute | solution.py:17
  5.9 1.8 %collective-permute-start.2 = (bf16[96,512]{1,0:T(8,128)(2,1)S(1)}, bf16[96,512]{1,0:T(8,128)(2,1)S(1)}, u32[]{:S(2)}, u32[]{:S(2)}) collective-permute-start(bf16[96,512]{1,0:T(8,128)(2,1)S(1)} %pad_maximum_fusion.13), channel_id=1, source_target_pairs={{0,3},{1,2},{2,1},{3,0},{4,7},{5,6},{6,5},{7,4},{8,11},{9,10},{10,... | collective-permute-start | bytes 294920 | tf_op jit(solution)/shard_map/ppermute | solution.py:17
  7.7 0.7 copy-done.7
  8.4 0.6 copy-done.6
  9.1 1.1 %collective-permute-done.1 = bf16[96,512]{1,0:T(8,128)(2,1)S(1)} collective-permute-done((bf16[96,512]{1,0:T(8,128)(2,1)S(1)}, bf16[96,512]{1,0:T(8,128)(2,1)S(1)}, u32[]{:S(2)}, u32[]{:S(2)}) %collective-permute-start.1) | collective-permute-done | bytes 98336 | tf_op jit(solution)/shard_map/ppermute | solution.py:17
  10.2 2.3 %collective-permute-done.2 = bf16[96,512]{1,0:T(8,128)(2,1)S(1)} collective-permute-done((bf16[96,512]{1,0:T(8,128)(2,1)S(1)}, bf16[96,512]{1,0:T(8,128)(2,1)S(1)}, u32[]{:S(2)}, u32[]{:S(2)}) %collective-permute-start.2) | collective-permute-done | bytes 98336 | tf_op jit(solution)/shard_map/ppermute | solution.py:17
  15.3 1.1 %pad_maximum_fusion = bf16[256,8,128]{2,1,0:T(8,128)(2,1)} fusion(bf16[256,4,128]{2,1,0:T(4,128)(2,1)S(1)} %reshape.143, bf16[256,4,128]{2,1,0:T(4,128)(2,1)S(1)} %reshape.142), kind=kLoop, calls=%fused_computation.22 | loop fusion | flops 1048576 | bytes 1048576 | tf_op jit(solution)/shard_map/concatenate | solution.py:63
  16.3 12.6 %all-to-all-start = ((bf16[256,8,128]{2,1,0:T(8,128)(2,1)}), bf16[256,8,128]{2,1,0:T(8,128)(2,1)S(1)}, u32[]{:S(2)}, u32[]{:S(2)}) async-start(bf16[256,8,128]{2,1,0:T(8,128)(2,1)} %pad_maximum_fusion), calls=%async_computation | async-start | bytes 1048576 | tf_op jit(solution)/shard_map/all_to_all | solution.py:66
  29.0 0.7 copy-done.5
  29.7 7.5 %all_gather.3 = bf16[128,256]{1,0:T(8,128)(2,1)S(1)} all-gather(bf16[32,256]{1,0:T(8,128)(2,1)S(1)} %pad_maximum_fusion.14), channel_id=1, replica_groups=mesh['row'=64,'ch'=4] {'ch'}, dimensions={0}, use_global_device_ids=true | all-gather | bytes 81920 | tf_op jit(solution)/shard_map/all_gather | solution.py:44
  37.2 12.9 %all-to-all-done = bf16[256,8,128]{2,1,0:T(8,128)(2,1)S(1)} async-done(((bf16[256,8,128]{2,1,0:T(8,128)(2,1)}), bf16[256,8,128]{2,1,0:T(8,128)(2,1)S(1)}, u32[]{:S(2)}, u32[]{:S(2)}) %all-to-all-start) | async-done | bytes 524320 | tf_op jit(solution)/shard_map/all_to_all | solution.py:66
  52.4 1.2 %pad_maximum_fusion.1 = bf16[256,2,512]{2,1,0:T(2,128)(2,1)S(1)} fusion(bf16[256,1,512]{2,1,0:T(2,128)(2,1)S(1)} %select_n.100, bf16[256,1,512]{2,1,0:T(2,128)(2,1)S(1)} %select_n.99), kind=kLoop, calls=%fused_computation.23 | loop fusion | flops 1048576 | bytes 1048576 | tf_op jit(solution)/shard_map/stack | solution.py:70
  54.2 1.1 %pad_maximum_fusion.2 = bf16[256,8,128]{2,1,0:T(8,128)(2,1)} fusion(bf16[256,4,128]{2,1,0:T(4,128)(2,1)S(1)} %bitcast.119, bf16[256,4,128]{2,1,0:T(4,128)(2,1)S(1)} %reshape.146), kind=kLoop, calls=%fused_computation.24 | loop fusion | flops 1048576 | bytes 1048576 | tf_op jit(solution)/shard_map/concatenate | solution.py:80
  55.3 5.3 %all-to-all-start.1 = ((bf16[256,8,128]{2,1,0:T(8,128)(2,1)}), bf16[256,8,128]{2,1,0:T(8,128)(2,1)S(1)}, u32[]{:S(2)}, u32[]{:S(2)}) async-start(bf16[256,8,128]{2,1,0:T(8,128)(2,1)} %pad_maximum_fusion.2), calls=%async_computation.1 | async-start | bytes 1048576 | tf_op jit(solution)/shard_map/all_to_all | solution.py:81
  60.7 21.1 %all-to-all-done.1 = bf16[256,8,128]{2,1,0:T(8,128)(2,1)S(1)} async-done(((bf16[256,8,128]{2,1,0:T(8,128)(2,1)}), bf16[256,8,128]{2,1,0:T(8,128)(2,1)S(1)}, u32[]{:S(2)}, u32[]{:S(2)}) %all-to-all-start.1) | async-done | bytes 524320 | tf_op jit(solution)/shard_map/all_to_all | solution.py:81
  83.0 0.6 copy-done.8
  83.9 0.6 collective-permute-start.6
  84.5 1.1 %collective-permute-start.5 = (bf16[2,32,512]{2,1,0:T(8,128)(2,1)S(1)}, bf16[2,32,512]{2,1,0:T(8,128)(2,1)S(1)}, u32[]{:S(2)}, u32[]{:S(2)}) collective-permute-start(bf16[2,32,512]{2,1,0:T(8,128)(2,1)S(1)} %get-tuple-element.22), channel_id=1, source_target_pairs={{0,2},{1,3},{2,0},{3,1},{4,6},{5,7},{6,4},{7,5},{8,10},{9,11},{10,... | collective-permute-start | bytes 196616 | tf_op jit(solution)/shard_map/ppermute | solution.py:17
  85.6 0.6 collective-permute-start.4
  86.2 2.2 %collective-permute-done.6 = bf16[2,32,512]{2,1,0:T(8,128)(2,1)S(1)} collective-permute-done((bf16[2,32,512]{2,1,0:T(8,128)(2,1)S(1)}, bf16[2,32,512]{2,1,0:T(8,128)(2,1)S(1)}, u32[]{:S(2)}, u32[]{:S(2)}) %collective-permute-start.6) | collective-permute-done | bytes 65568 | tf_op jit(solution)/shard_map/ppermute | solution.py:17
  88.3 0.9 %collective-permute-done.5 = bf16[2,32,512]{2,1,0:T(8,128)(2,1)S(1)} collective-permute-done((bf16[2,32,512]{2,1,0:T(8,128)(2,1)S(1)}, bf16[2,32,512]{2,1,0:T(8,128)(2,1)S(1)}, u32[]{:S(2)}, u32[]{:S(2)}) %collective-permute-start.5) | collective-permute-done | bytes 65568 | tf_op jit(solution)/shard_map/ppermute | solution.py:17
  89.4 0.9 copy.101
  (73 shorter events, 7.5 us)
Async XLA Ops:
  1.7 0.7 copy-start.1
  1.7 0.7 copy-start.2
  1.7 0.7 copy-start.3
  1.8 0.7 copy-start
  2.5 6.6 %collective-permute-start = (bf16[96,512]{1,0:T(8,128)(2,1)S(1)}, bf16[96,512]{1,0:T(8,128)(2,1)S(1)}, u32[]{:S(2)}, u32[]{:S(2)}) collective-permute-start(bf16[96,512]{1,0:T(8,128)(2,1)S(1)} %get-tuple-element.33), channel_id=1, source_target_pairs={{0,1},{1,0},{2,3},{3,2},{4,5},{5,4},{6,7},{7,6},{8,9},{9,8},{10,11... | collective-permute-start | bytes 294920 | tf_op jit(solution)/shard_map/ppermute | solution.py:17
  5.8 4.4 %collective-permute-start.1 = (bf16[96,512]{1,0:T(8,128)(2,1)S(1)}, bf16[96,512]{1,0:T(8,128)(2,1)S(1)}, u32[]{:S(2)}, u32[]{:S(2)}) collective-permute-start(bf16[96,512]{1,0:T(8,128)(2,1)S(1)} %get-tuple-element.34), channel_id=1, source_target_pairs={{0,2},{1,3},{2,0},{3,1},{4,6},{5,7},{6,4},{7,5},{8,10},{9,11},{10,... | collective-permute-start | bytes 294920 | tf_op jit(solution)/shard_map/ppermute | solution.py:17
  5.9 6.6 %collective-permute-start.2 = (bf16[96,512]{1,0:T(8,128)(2,1)S(1)}, bf16[96,512]{1,0:T(8,128)(2,1)S(1)}, u32[]{:S(2)}, u32[]{:S(2)}) collective-permute-start(bf16[96,512]{1,0:T(8,128)(2,1)S(1)} %pad_maximum_fusion.13), channel_id=1, source_target_pairs={{0,3},{1,2},{2,1},{3,0},{4,7},{5,6},{6,5},{7,4},{8,11},{9,10},{10,... | collective-permute-start | bytes 294920 | tf_op jit(solution)/shard_map/ppermute | solution.py:17
  7.7 0.7 copy-start.7
  8.3 0.7 copy-start.6
  16.3 33.7 %all-to-all-start = ((bf16[256,8,128]{2,1,0:T(8,128)(2,1)}), bf16[256,8,128]{2,1,0:T(8,128)(2,1)S(1)}, u32[]{:S(2)}, u32[]{:S(2)}) async-start(bf16[256,8,128]{2,1,0:T(8,128)(2,1)} %pad_maximum_fusion), calls=%async_computation | async-start | bytes 1048576 | tf_op jit(solution)/shard_map/all_to_all | solution.py:66
  29.0 0.7 copy-start.5
  29.0 0.7 copy-start.4
  50.1 1.6 %collective-permute-start.3 = (bf16[256,4,128]{2,1,0:T(4,128)(2,1)S(1)}, bf16[256,4,128]{2,1,0:T(4,128)(2,1)S(1)}, u32[]{:S(2)}, u32[]{:S(2)}) collective-permute-start(bf16[256,4,128]{2,1,0:T(4,128)(2,1)S(1)} %slice.55), channel_id=1, source_target_pairs={{0,1},{1,0},{2,3},{3,2},{4,5},{5,4},{6,7},{7,6},{8,9},{9,8},{10,11... | collective-permute-start | bytes 786440 | tf_op jit(solution)/shard_map/ppermute | solution.py:17
  55.3 26.5 %all-to-all-start.1 = ((bf16[256,8,128]{2,1,0:T(8,128)(2,1)}), bf16[256,8,128]{2,1,0:T(8,128)(2,1)S(1)}, u32[]{:S(2)}, u32[]{:S(2)}) async-start(bf16[256,8,128]{2,1,0:T(8,128)(2,1)} %pad_maximum_fusion.2), calls=%async_computation.1 | async-start | bytes 1048576 | tf_op jit(solution)/shard_map/all_to_all | solution.py:81
  82.9 0.7 copy-start.8
  82.9 0.7 copy-start.9
  83.9 4.4 %collective-permute-start.6 = (bf16[2,32,512]{2,1,0:T(8,128)(2,1)S(1)}, bf16[2,32,512]{2,1,0:T(8,128)(2,1)S(1)}, u32[]{:S(2)}, u32[]{:S(2)}) collective-permute-start(bf16[2,32,512]{2,1,0:T(8,128)(2,1)S(1)} %get-tuple-element.21), channel_id=1, source_target_pairs={{0,3},{1,2},{2,1},{3,0},{4,7},{5,6},{6,5},{7,4},{8,11},{9,10},{10,... | collective-permute-start | bytes 196616 | tf_op jit(solution)/shard_map/ppermute | solution.py:17
  84.5 4.8 %collective-permute-start.5 = (bf16[2,32,512]{2,1,0:T(8,128)(2,1)S(1)}, bf16[2,32,512]{2,1,0:T(8,128)(2,1)S(1)}, u32[]{:S(2)}, u32[]{:S(2)}) collective-permute-start(bf16[2,32,512]{2,1,0:T(8,128)(2,1)S(1)} %get-tuple-element.22), channel_id=1, source_target_pairs={{0,2},{1,3},{2,0},{3,1},{4,6},{5,7},{6,4},{7,5},{8,10},{9,11},{10,... | collective-permute-start | bytes 196616 | tf_op jit(solution)/shard_map/ppermute | solution.py:17
  85.6 3.7 %collective-permute-start.4 = (bf16[2,32,512]{2,1,0:T(8,128)(2,1)S(1)}, bf16[2,32,512]{2,1,0:T(8,128)(2,1)S(1)}, u32[]{:S(2)}, u32[]{:S(2)}) collective-permute-start(bf16[2,32,512]{2,1,0:T(8,128)(2,1)S(1)} %get-tuple-element.23), channel_id=1, source_target_pairs={{0,1},{1,0},{2,3},{3,2},{4,5},{5,4},{6,7},{7,6},{8,9},{9,8},{10,11... | collective-permute-start | bytes 196616 | tf_op jit(solution)/shard_map/ppermute | solution.py:17
where the time goes:
time: 90.7 us; the launch traced here: 90.2 us
  waiting for transfers between devices  40.9 us (45%)
  starting transfers between devices  25.6 us (28%)
  local copies, waits for them, and re-layouts  8.92 us (10%)
  blocking collectives  7.46 us (8%)
  other arithmetic  4.84 us (5%)
  matrix products  1.97 us (2%)
    all_to_all x1, waiting for transfers between devices, body(): got = lax.all_to_all(sent, everyone, 0, 0, tiled=True)  21.1 us
    all_to_all x1, waiting for transfers between devices, body(): factors = lax.all_to_all(sent, everyone, 0, 0, tiled=True)  12.9 us
    all_to_all x1, starting transfers between devices, body(): factors = lax.all_to_all(sent, everyone, 0, 0, tiled=True)  12.6 us
    ppermute x7, starting transfers between devices, swap(): return lax.ppermute(array, 'ch', [(s, s ^ step) for s in range(4)])  7.68 us
    all_gather x1, blocking collectives, body(): lax.all_gather(jnp.concatenate([gate_weight.T, final_weight.T], axis=1),...  7.46 us
    ppermute x7, waiting for transfers between devices, swap(): return lax.ppermute(array, 'ch', [(s, s ^ step) for s in range(4)])  6.98 us
    all_to_all x1, starting transfers between devices, body(): got = lax.all_to_all(sent, everyone, 0, 0, tiled=True)  5.33 us
    unnamed x24, local copies, waits for them, and re-layouts  3.31 us
  transfers between devices with their start and end apart: 9, of which 7 were waited for; matrix products, arithmetic and copies ran while one was open for 1% of the time, Pallas kernels for 0%

commit v1 on v0

--- a/solution.py
+++ b/solution.py
@@ -41,8 +41,16 @@
     weights = jnp.concatenate(
         [w.T for w in (left_weight, left_gate, right_weight, right_gate)], axis=1
     )
-    late = lax.all_gather(
-        jnp.concatenate([gate_weight.T, final_weight.T], axis=1), "ch", axis=0, tiled=True
+    late = jnp.concatenate(
+        lax.all_to_all(
+            jnp.stack(
+                [jnp.concatenate([gate_weight.T, final_weight.T], axis=1)] * lax.axis_size("ch")
+            ),
+            "ch",
+            0,
+            0,
+        ),
+        axis=0,
     )
     field = jnp.swapaxes(pair_field, 0, 1)
 

time: 90.7 us -> 97.7 us (1.077)
  waiting for transfers between devices: 40.9 us -> 50.8 us
  blocking collectives: 7.46 us -> 0 us
  starting transfers between devices: 25.6 us -> 29.5 us
    all_gather x1 -> x0, blocking collectives: 7.46 us -> none  [body(): lax.all_gather(jnp.concatenate([gate_weight.T, final_weight.T], axis=1),...]
    all_to_all x1, waiting for transfers between devices: 12.9 us -> 20.3 us  [body(): factors = lax.all_to_all(sent, everyone, 0, 0, tiled=True)]
    all_to_all x0 -> x1, starting transfers between devices: none -> 3.48 us  [body(): lax.all_to_all(jnp.stack([jnp.concatenate([gate_weight.T, final_weight.T]...]
    all_to_all x0 -> x1, waiting for transfers between devices: none -> 2.85 us  [body(): lax.all_to_all(jnp.stack([jnp.concatenate([gate_weight.T, final_weight.T]...]
    another operation x3 -> x4, local copies, waits for them, and re-layouts: 2.22 us -> 2.85 us
  transfers between devices with their start and end apart: 9 -> 10, of which waited for: 7 -> 7; matrix products, arithmetic and copies ran while one was open for 1% -> 1% of each run, Pallas kernels for 0% -> 0%
where the time goes in v1:
time: 97.7 us; the launch traced here: 97.2 us
  waiting for transfers between devices  50.8 us (52%)
  starting transfers between devices  29.5 us (30%)
  local copies, waits for them, and re-layouts  9.56 us (10%)
  other arithmetic  4.82 us (5%)
  matrix products  1.98 us (2%)
    all_to_all x1, waiting for transfers between devices, body(): got = lax.all_to_all(sent, everyone, 0, 0, tiled=True)  21.2 us
    all_to_all x1, waiting for transfers between devices, body(): factors = lax.all_to_all(sent, everyone, 0, 0, tiled=True)  20.3 us
    all_to_all x1, starting transfers between devices, body(): factors = lax.all_to_all(sent, everyone, 0, 0, tiled=True)  12.6 us
    ppermute x7, starting transfers between devices, swap(): return lax.ppermute(array, 'ch', [(s, s ^ step) for s in range(4)])  7.5 us
    ppermute x7, waiting for transfers between devices, swap(): return lax.ppermute(array, 'ch', [(s, s ^ step) for s in range(4)])  6.5 us
    all_to_all x1, starting transfers between devices, body(): got = lax.all_to_all(sent, everyone, 0, 0, tiled=True)  5.89 us
    all_to_all x1, starting transfers between devices, body(): lax.all_to_all(jnp.stack([jnp.concatenate([gate_weight.T, final_weight.T]...  3.48 us
    unnamed x24, local copies, waits for them, and re-layouts  3.31 us
  transfers between devices with their start and end apart: 10, of which 7 were waited for; matrix products, arithmetic and copies ran while one was open for 1% of the time, Pallas kernels for 0%

profile of v1, /device:TPU:1, one launch (start us, length us, event | category | flops | bytes accessed | tf_op | source)
XLA Modules:
  0.0 97.2 jit_solution(15726027051890271585)
XLA Ops:
  0.0 1.7 %constant_dynamic-slice_fusion.14 = (bf16[32,2,512]{2,1,0:T(2,128)(2,1)S(1)}, bf16[32,2,512]{2,1,0:T(2,128)(2,1)S(1)}, bf16[32,2,512]{2,1,0:T(2,128)(2,1)S(1)}, bf16[32,2,512]{2,1,0:T(2,128)(2,1)S(1)}) fusion(bf16[32,8,512]{2,1,0:T(8,128)(2,1)} %param.11, s32[]{:T(128)S(6)} %select_n.81, s32[]{:T(128)S(6)} %select_n.83, s32[]{:T(128)S(6)} %select_n.82, ...), kind=kLoop, calls=%fused_computation.85 | loop fusion | bytes 524304 | tf_op jit(solution)/shard_map/dynamic-slice
  1.8 0.6 copy-done.1
  2.5 3.3 %collective-permute-start = (bf16[96,512]{1,0:T(8,128)(2,1)S(1)}, bf16[96,512]{1,0:T(8,128)(2,1)S(1)}, u32[]{:S(2)}, u32[]{:S(2)}) collective-permute-start(bf16[96,512]{1,0:T(8,128)(2,1)S(1)} %get-tuple-element.33), channel_id=1, source_target_pairs={{0,1},{1,0},{2,3},{3,2},{4,5},{5,4},{6,7},{7,6},{8,9},{9,8},{10,11... | collective-permute-start | bytes 294920 | tf_op jit(solution)/shard_map/ppermute | solution.py:17
  5.9 1.8 %collective-permute-start.2 = (bf16[96,512]{1,0:T(8,128)(2,1)S(1)}, bf16[96,512]{1,0:T(8,128)(2,1)S(1)}, u32[]{:S(2)}, u32[]{:S(2)}) collective-permute-start(bf16[96,512]{1,0:T(8,128)(2,1)S(1)} %pad_maximum_fusion.13), channel_id=1, source_target_pairs={{0,3},{1,2},{2,1},{3,0},{4,7},{5,6},{6,5},{7,4},{8,11},{9,10},{10,... | collective-permute-start | bytes 294920 | tf_op jit(solution)/shard_map/ppermute | solution.py:17
  7.7 0.7 copy-done.7
  8.4 0.6 copy-done.6
  9.1 1.1 %collective-permute-done.1 = bf16[96,512]{1,0:T(8,128)(2,1)S(1)} collective-permute-done((bf16[96,512]{1,0:T(8,128)(2,1)S(1)}, bf16[96,512]{1,0:T(8,128)(2,1)S(1)}, u32[]{:S(2)}, u32[]{:S(2)}) %collective-permute-start.1) | collective-permute-done | bytes 98336 | tf_op jit(solution)/shard_map/ppermute | solution.py:17
  10.2 2.3 %collective-permute-done.2 = bf16[96,512]{1,0:T(8,128)(2,1)S(1)} collective-permute-done((bf16[96,512]{1,0:T(8,128)(2,1)S(1)}, bf16[96,512]{1,0:T(8,128)(2,1)S(1)}, u32[]{:S(2)}, u32[]{:S(2)}) %collective-permute-start.2) | collective-permute-done | bytes 98336 | tf_op jit(solution)/shard_map/ppermute | solution.py:17
  15.3 1.1 %pad_maximum_fusion = bf16[256,8,128]{2,1,0:T(8,128)(2,1)} fusion(bf16[256,4,128]{2,1,0:T(4,128)(2,1)S(1)} %reshape.148, bf16[256,4,128]{2,1,0:T(4,128)(2,1)S(1)} %reshape.147), kind=kLoop, calls=%fused_computation.22 | loop fusion | flops 1048576 | bytes 1048576 | tf_op jit(solution)/shard_map/concatenate | solution.py:71
  16.3 12.6 %all-to-all-start = ((bf16[256,8,128]{2,1,0:T(8,128)(2,1)}), bf16[256,8,128]{2,1,0:T(8,128)(2,1)S(1)}, u32[]{:S(2)}, u32[]{:S(2)}) async-start(bf16[256,8,128]{2,1,0:T(8,128)(2,1)} %pad_maximum_fusion), calls=%async_computation | async-start | bytes 1048576 | tf_op jit(solution)/shard_map/all_to_all | solution.py:74
  29.0 0.7 copy-done.5
  29.7 20.3 %all-to-all-done = bf16[256,8,128]{2,1,0:T(8,128)(2,1)S(1)} async-done(((bf16[256,8,128]{2,1,0:T(8,128)(2,1)}), bf16[256,8,128]{2,1,0:T(8,128)(2,1)S(1)}, u32[]{:S(2)}, u32[]{:S(2)}) %all-to-all-start) | async-done | bytes 524320 | tf_op jit(solution)/shard_map/all_to_all | solution.py:74
  50.0 0.6 stack.63
  50.7 3.5 %all-to-all-start.1 = ((bf16[4,32,256]{2,1,0:T(8,128)(2,1)}), bf16[4,32,256]{2,1,0:T(8,128)(2,1)S(1)}, u32[]{:S(2)}, u32[]{:S(2)}) async-start(bf16[4,32,256]{2,1,0:T(8,128)(2,1)} %stack.63), calls=%async_computation.1 | async-start | bytes 131072 | tf_op jit(solution)/shard_map/all_to_all | solution.py:45
  54.6 2.8 %all-to-all-done.1 = bf16[4,32,256]{2,1,0:T(8,128)(2,1)S(1)} async-done(((bf16[4,32,256]{2,1,0:T(8,128)(2,1)}), bf16[4,32,256]{2,1,0:T(8,128)(2,1)S(1)}, u32[]{:S(2)}, u32[]{:S(2)}) %all-to-all-start.1) | async-done | bytes 65568 | tf_op jit(solution)/shard_map/all_to_all | solution.py:45
  58.7 1.2 %pad_maximum_fusion.1 = bf16[256,2,512]{2,1,0:T(2,128)(2,1)S(1)} fusion(bf16[256,1,512]{2,1,0:T(2,128)(2,1)S(1)} %select_n.100, bf16[256,1,512]{2,1,0:T(2,128)(2,1)S(1)} %select_n.99), kind=kLoop, calls=%fused_computation.23 | loop fusion | flops 1048576 | bytes 1048576 | tf_op jit(solution)/shard_map/stack | solution.py:78
  60.5 1.1 %pad_maximum_fusion.2 = bf16[256,8,128]{2,1,0:T(8,128)(2,1)} fusion(bf16[256,4,128]{2,1,0:T(4,128)(2,1)S(1)} %bitcast.120, bf16[256,4,128]{2,1,0:T(4,128)(2,1)S(1)} %reshape.151), kind=kLoop, calls=%fused_computation.24 | loop fusion | flops 1048576 | bytes 1048576 | tf_op jit(solution)/shard_map/concatenate | solution.py:88
  61.6 5.9 %all-to-all-start.2 = ((bf16[256,8,128]{2,1,0:T(8,128)(2,1)}), bf16[256,8,128]{2,1,0:T(8,128)(2,1)S(1)}, u32[]{:S(2)}, u32[]{:S(2)}) async-start(bf16[256,8,128]{2,1,0:T(8,128)(2,1)} %pad_maximum_fusion.2), calls=%async_computation.2 | async-start | bytes 1048576 | tf_op jit(solution)/shard_map/all_to_all | solution.py:89
  67.5 21.2 %all-to-all-done.2 = bf16[256,8,128]{2,1,0:T(8,128)(2,1)S(1)} async-done(((bf16[256,8,128]{2,1,0:T(8,128)(2,1)}), bf16[256,8,128]{2,1,0:T(8,128)(2,1)S(1)}, u32[]{:S(2)}, u32[]{:S(2)}) %all-to-all-start.2) | async-done | bytes 524320 | tf_op jit(solution)/shard_map/all_to_all | solution.py:89
  89.9 0.6 copy-done.8
  91.4 1.1 %collective-permute-start.5 = (bf16[2,32,512]{2,1,0:T(8,128)(2,1)S(1)}, bf16[2,32,512]{2,1,0:T(8,128)(2,1)S(1)}, u32[]{:S(2)}, u32[]{:S(2)}) collective-permute-start(bf16[2,32,512]{2,1,0:T(8,128)(2,1)S(1)} %get-tuple-element.22), channel_id=1, source_target_pairs={{0,2},{1,3},{2,0},{3,1},{4,6},{5,7},{6,4},{7,5},{8,10},{9,11},{10,... | collective-permute-start | bytes 196616 | tf_op jit(solution)/shard_map/ppermute | solution.py:17
  93.1 2.2 %collective-permute-done.6 = bf16[2,32,512]{2,1,0:T(8,128)(2,1)S(1)} collective-permute-done((bf16[2,32,512]{2,1,0:T(8,128)(2,1)S(1)}, bf16[2,32,512]{2,1,0:T(8,128)(2,1)S(1)}, u32[]{:S(2)}, u32[]{:S(2)}) %collective-permute-start.6) | collective-permute-done | bytes 65568 | tf_op jit(solution)/shard_map/ppermute | solution.py:17
  95.3 0.9 collective-permute-done.5
  96.3 0.9 copy.101
  (75 shorter events, 8.0 us)
Async XLA Ops:
  1.7 0.7 copy-start.1
  1.7 0.7 copy-start.2
  1.7 0.7 copy-start.3
  1.8 0.7 copy-start
  2.5 6.6 %collective-permute-start = (bf16[96,512]{1,0:T(8,128)(2,1)S(1)}, bf16[96,512]{1,0:T(8,128)(2,1)S(1)}, u32[]{:S(2)}, u32[]{:S(2)}) collective-permute-start(bf16[96,512]{1,0:T(8,128)(2,1)S(1)} %get-tuple-element.33), channel_id=1, source_target_pairs={{0,1},{1,0},{2,3},{3,2},{4,5},{5,4},{6,7},{7,6},{8,9},{9,8},{10,11... | collective-permute-start | bytes 294920 | tf_op jit(solution)/shard_map/ppermute | solution.py:17
  5.8 4.4 %collective-permute-start.1 = (bf16[96,512]{1,0:T(8,128)(2,1)S(1)}, bf16[96,512]{1,0:T(8,128)(2,1)S(1)}, u32[]{:S(2)}, u32[]{:S(2)}) collective-permute-start(bf16[96,512]{1,0:T(8,128)(2,1)S(1)} %get-tuple-element.34), channel_id=1, source_target_pairs={{0,2},{1,3},{2,0},{3,1},{4,6},{5,7},{6,4},{7,5},{8,10},{9,11},{10,... | collective-permute-start | bytes 294920 | tf_op jit(solution)/shard_map/ppermute | solution.py:17
  5.9 6.6 %collective-permute-start.2 = (bf16[96,512]{1,0:T(8,128)(2,1)S(1)}, bf16[96,512]{1,0:T(8,128)(2,1)S(1)}, u32[]{:S(2)}, u32[]{:S(2)}) collective-permute-start(bf16[96,512]{1,0:T(8,128)(2,1)S(1)} %pad_maximum_fusion.13), channel_id=1, source_target_pairs={{0,3},{1,2},{2,1},{3,0},{4,7},{5,6},{6,5},{7,4},{8,11},{9,10},{10,... | collective-permute-start | bytes 294920 | tf_op jit(solution)/shard_map/ppermute | solution.py:17
  7.7 0.7 copy-start.7
  8.3 0.7 copy-start.6
  16.3 33.7 %all-to-all-start = ((bf16[256,8,128]{2,1,0:T(8,128)(2,1)}), bf16[256,8,128]{2,1,0:T(8,128)(2,1)S(1)}, u32[]{:S(2)}, u32[]{:S(2)}) async-start(bf16[256,8,128]{2,1,0:T(8,128)(2,1)} %pad_maximum_fusion), calls=%async_computation | async-start | bytes 1048576 | tf_op jit(solution)/shard_map/all_to_all | solution.py:74
  29.0 0.7 copy-start.5
  29.0 0.7 copy-start.4
  50.7 6.7 %all-to-all-start.1 = ((bf16[4,32,256]{2,1,0:T(8,128)(2,1)}), bf16[4,32,256]{2,1,0:T(8,128)(2,1)S(1)}, u32[]{:S(2)}, u32[]{:S(2)}) async-start(bf16[4,32,256]{2,1,0:T(8,128)(2,1)} %stack.63), calls=%async_computation.1 | async-start | bytes 131072 | tf_op jit(solution)/shard_map/all_to_all | solution.py:45
  54.2 3.8 %collective-permute-start.3 = (bf16[256,4,128]{2,1,0:T(4,128)(2,1)S(1)}, bf16[256,4,128]{2,1,0:T(4,128)(2,1)S(1)}, u32[]{:S(2)}, u32[]{:S(2)}) collective-permute-start(bf16[256,4,128]{2,1,0:T(4,128)(2,1)S(1)} %slice.55), channel_id=1, source_target_pairs={{0,1},{1,0},{2,3},{3,2},{4,5},{5,4},{6,7},{7,6},{8,9},{9,8},{10,11... | collective-permute-start | bytes 786440 | tf_op jit(solution)/shard_map/ppermute | solution.py:17
  61.6 27.1 %all-to-all-start.2 = ((bf16[256,8,128]{2,1,0:T(8,128)(2,1)}), bf16[256,8,128]{2,1,0:T(8,128)(2,1)S(1)}, u32[]{:S(2)}, u32[]{:S(2)}) async-start(bf16[256,8,128]{2,1,0:T(8,128)(2,1)} %pad_maximum_fusion.2), calls=%async_computation.2 | async-start | bytes 1048576 | tf_op jit(solution)/shard_map/all_to_all | solution.py:89
  89.8 0.7 copy-start.8
  89.8 0.7 copy-start.9
  90.9 4.4 %collective-permute-start.6 = (bf16[2,32,512]{2,1,0:T(8,128)(2,1)S(1)}, bf16[2,32,512]{2,1,0:T(8,128)(2,1)S(1)}, u32[]{:S(2)}, u32[]{:S(2)}) collective-permute-start(bf16[2,32,512]{2,1,0:T(8,128)(2,1)S(1)} %get-tuple-element.21), channel_id=1, source_target_pairs={{0,3},{1,2},{2,1},{3,0},{4,7},{5,6},{6,5},{7,4},{8,11},{9,10},{10,... | collective-permute-start | bytes 196616 | tf_op jit(solution)/shard_map/ppermute | solution.py:17
  91.4 4.8 %collective-permute-start.5 = (bf16[2,32,512]{2,1,0:T(8,128)(2,1)S(1)}, bf16[2,32,512]{2,1,0:T(8,128)(2,1)S(1)}, u32[]{:S(2)}, u32[]{:S(2)}) collective-permute-start(bf16[2,32,512]{2,1,0:T(8,128)(2,1)S(1)} %get-tuple-element.22), channel_id=1, source_target_pairs={{0,2},{1,3},{2,0},{3,1},{4,6},{5,7},{6,4},{7,5},{8,10},{9,11},{10,... | collective-permute-start | bytes 196616 | tf_op jit(solution)/shard_map/ppermute | solution.py:17
  92.5 3.7 %collective-permute-start.4 = (bf16[2,32,512]{2,1,0:T(8,128)(2,1)S(1)}, bf16[2,32,512]{2,1,0:T(8,128)(2,1)S(1)}, u32[]{:S(2)}, u32[]{:S(2)}) collective-permute-start(bf16[2,32,512]{2,1,0:T(8,128)(2,1)S(1)} %get-tuple-element.23), channel_id=1, source_target_pairs={{0,1},{1,0},{2,3},{3,2},{4,5},{5,4},{6,7},{7,6},{8,9},{9,8},{10,11... | collective-permute-start | bytes 196616 | tf_op jit(solution)/shard_map/ppermute | solution.py:17
